TPU v7x, 256 devices: a whole 4x4x8 slice. The times are simulated.
256 devices in a mesh: row: 8 (over z), col: 16 (over y, x), layer: 2 (over core).
Axes of the slice: x: 4, y: 4, z: 8, core: 2. Of those that a mesh axis runs over, the one named last changes fastest.
Arguments:
- density: bfloat16 [8192, 8192], P('row', ('col', 'layer')), may hold values from -3 to 3
- block_mask: int32 [64, 64], P('row', ('col', 'layer')), may hold values from 0 to 1, as said below
- keep_mask: int32 [64, 64], P('row', ('col', 'layer')), may hold values 0 or 1
- branch_flag: int32 [64], P('row'), may hold values from 0 to 1
Outputs:
- updated: float32 [8192, 8192], P('row', ('col', 'layer'))
- trace_new: float32 [], replicated
Inputs may be any that keep to these rules, and one draw needn't show every extreme that they name: `block_mask`: symmetric, 1 on the diagonal; 1 where two blocks' centres in a periodic box lie within a cutoff distance of each other, else 0; block labels are in no spatial order. `keep_mask`: 0 or 1 for each block.
All inputs are finite; a program needn't handle non-finite values.
Results may differ from a plain program's by a relative error of at most 0.0004.
Values may be sent and summed in bfloat16 or wider, within the bound.
No kernel may reach another device: no remote copies, remote signals or barrier semaphores. Data moves between devices by JAX's collectives and lax.ppermute only.
A program may use at most 64 MiB of HBM per device.

v0:
```python
import functools
import jax
import jax.numpy as jnp
from jax import lax
from jax.sharding import Mesh
from jax.sharding import PartitionSpec as P

BLK = 128
COL = ("col_0", "col_1")
ROW_COL_LAYER = ("row", "col_0", "col_1", "layer")
COL_LAYER = ("col_0", "col_1", "layer")


def partner(value, axis, stride):
    mask = 2**stride
    pairs = [(source, source ^ mask) for source in range(lax.axis_size(axis))]
    return lax.ppermute(value, axis, pairs)


def split_up(value, dim, devices):
    shape = value.shape
    pieces = value.reshape(*shape[:dim], devices, shape[dim] // devices, *shape[dim + 1 :])
    return jnp.moveaxis(pieces, dim, 0)


def sum_at_owner(value, axis, dim):
    devices = lax.axis_size(axis)
    pieces = lax.all_to_all(split_up(value, dim, devices), axis, 0, 0, tiled=True)
    return jnp.sum(pieces, axis=0)


def over_axes(value, axes):
    return functools.reduce(lax.psum, axes, value)


def expand_mask(block_mask):
    return jnp.repeat(jnp.repeat(block_mask, BLK, axis=0), BLK, axis=1)


def on_device(density, block_mask, keep_mask, branch_flag):
    row_count = density.shape[0]
    col_width = density.shape[1]
    masked = density * expand_mask(block_mask).astype(jnp.bfloat16)
    col_panel = lax.all_gather(masked, "row", axis=0, tiled=True)
    layer_index = lax.axis_index("layer")
    col_groups = lax.axis_size(COL)
    grouped = col_panel.reshape(col_groups, 2, col_width, col_width)
    own_rows = lax.dynamic_index_in_dim(grouped, layer_index, 1, keepdims=False)
    outgoing = lax.dynamic_index_in_dim(grouped, 1 - layer_index, 1, keepdims=False)
    peer_rows = partner(outgoing, "layer", 0)
    own_rows = own_rows.reshape(col_groups * col_width, col_width)
    peer_rows = peer_rows.reshape(col_groups * col_width, col_width)
    lead_part = jnp.where(layer_index == 0, own_rows, peer_rows)
    tail_part = jnp.where(layer_index == 0, peer_rows, own_rows)
    inner_panel = jnp.concatenate([lead_part, tail_part], axis=1)
    partial_value = jnp.dot(
        lax.all_gather(masked, COL, axis=1, tiled=True),
        inner_panel,
        preferred_element_type=jnp.float32,
    )
    product = sum_at_owner(partial_value, "layer", 1)
    doubled = 2.0 * masked.astype(jnp.float32) - product
    flag_rows = jnp.repeat(branch_flag, BLK)[:, None]
    chosen = jnp.where(flag_rows == 1, product, doubled)
    updated = chosen * expand_mask(keep_mask).astype(jnp.float32)
    row_anchor = lax.axis_index("row") * row_count
    col_anchor = (
        lax.axis_index(COL) * lax.axis_size("layer") + lax.axis_index("layer")
    ) * col_width
    row_ids = row_anchor + jnp.arange(row_count, dtype=jnp.int32)[:, None]
    col_ids = col_anchor + jnp.arange(col_width, dtype=jnp.int32)[None, :]
    local_trace = jnp.sum(jnp.where(row_ids == col_ids, updated, 0.0))
    trace_new = over_axes(local_trace, ROW_COL_LAYER)
    return (updated, trace_new)


def solution(mesh):
    split = Mesh(
        mesh.devices.reshape(mesh.shape["row"], 4, 4, mesh.shape["layer"]),
        ("row", "col_0", "col_1", "layer"),
    )
    in_specs = (P("row", COL_LAYER), P("row", COL_LAYER), P("row", COL_LAYER), P("row"))
    out_specs = (P("row", COL_LAYER), P())
    return jax.shard_map(
        on_device, mesh=split, in_specs=in_specs, out_specs=out_specs, check_vma=False
    )
```

profile of v0, /device:TPU:1, one launch (start us, length us, event | category | flops | bytes accessed | tf_op | source)
XLA Modules:
  0.0 212.9 jit_solution(15898853218652076611)
XLA Ops:
  7.2 1.2 copy.10
  8.5 0.7 convert_element_type.25
  9.1 0.1 broadcast_bitcast_fusion.1
  9.2 0.8 bitcast_multiply_fusion
  10.1 0.7 all-gather.3.cloned.1.call-update
  10.9 58.0 %all-gather.5.cloned.1.call-done = bf16[8192,256]{0,1:T(8,128)(2,1)} async-done(((bf16[1024,256]{0,1:T(8,128)(2,1)}), bf16[8192,256]{0,1:T(8,128)(2,1)}) %all-gather.5.cloned.1.call-update) | async-done | bytes 4194320 | tf_op jit(solution)/shard_map/all_gather | solution.py:44
  68.9 7.8 %reshape.44 = bf16[16,2,256,256]{2,1,0,3:T(2,128)(2,1)} reshape(bf16[8192,256]{0,1:T(8,128)(2,1)} %all-gather.5.cloned.1.call-done) | data formatting | bytes 8388608 | tf_op jit(solution)/shard_map/reshape | solution.py:47
  76.7 13.4 %constant_dynamic-slice_fusion.1 = (bf16[16,1,256,256]{2,1,0,3:T(2,128)(2,1)}, bf16[16,1,256,256]{2,1,0,3:T(2,128)(2,1)}) fusion(bf16[16,2,256,256]{2,1,0,3:T(2,128)(2,1)} %reshape.44, s32[]{:T(128)S(6)} %select_n.28, s32[]{:T(128)S(6)} %select_n.29), kind=kLoop, calls=%fused_computation.18 | loop fusion | bytes 8388616 | tf_op jit(solution)/shard_map/jit(dynamic_index_in_dim)/dynamic_slice | solution.py:48
  90.1 10.5 %copy.15 = bf16[16,1,256,256]{3,2,0,1:T(8,128)(2,1)} copy(bf16[16,1,256,256]{2,1,0,3:T(2,128)(2,1)} %get-tuple-element.11) | data formatting | bytes 4194304
  100.6 0.7 collective-permute-start
  101.3 0.1 broadcast_bitcast_fusion
  101.4 0.1 broadcast_bitcast_fusion.2
  101.5 9.0 %copy.14 = bf16[16,1,256,256]{3,2,0,1:T(8,128)(2,1)S(1)} copy(bf16[16,1,256,256]{2,1,0,3:T(2,128)(2,1)} %get-tuple-element.10) | data formatting | bytes 4194304
  110.5 3.8 %bitcast_select_fusion.1 = (bf16[4096,256]{1,0:T(8,128)(2,1)}, bf16[4096,256]{1,0:T(8,128)(2,1)}) fusion(bf16[16,256,256]{2,1,0:T(8,128)(2,1)} %collective-permute-done, bf16[16,1,256,256]{3,2,0,1:T(8,128)(2,1)S(1)} %copy.14, pred[]{:T(512)S(6)} %eq.35), kind=kLoop, calls=%fused_computation.5 | loop fusion | flops 2097152 | bytes 8388609 | tf_op jit(solution)/shard_map/jit(_where)/select_n | solution.py:53
  114.3 31.4 %all-gather.3.cloned.1.call-done = bf16[1024,4096]{0,1:T(8,128)(2,1)} async-done(((bf16[1024,256]{0,1:T(8,128)(2,1)}), bf16[1024,4096]{0,1:T(8,128)(2,1)}) %all-gather.3.cloned.1.call-update) | async-done | bytes 8388624 | tf_op jit(solution)/shard_map/all_gather | solution.py:57
  145.7 8.3 %fusion = f32[1024,512]{0,1:T(8,128)S(1)} fusion(bf16[1024,4096]{0,1:T(8,128)(2,1)} %all-gather.3.cloned.1.call-done, bf16[4096,256]{1,0:T(8,128)(2,1)} %get-tuple-element.9, bf16[4096,256]{1,0:T(8,128)(2,1)} %get-tuple-element.8), kind=kOutput, calls=%fused_computation | convolution fusion | flops 4303355904 | bytes 14680064 | tf_op jit(solution)/shard_map/dot_general | solution.py:56
  154.0 5.8 %all_to_all.5 = f32[2,1024,256]{1,2,0:T(8,128)S(1)} all-to-all(f32[2,1024,256]{1,2,0:T(8,128)S(1)} %bitcast.34), channel_id=1, replica_groups=mesh['row'=8,'col_0'=4,'col_1'=4,'layer'=2] {'layer'}, dimensions={0} | all-to-all | bytes 4194304 | tf_op jit(solution)/shard_map/all_to_all | solution.py:28
  159.8 1.2 reduce_sum.18
  161.0 2.3 %select_reduce_fusion = (f32[]{:T(128)}, f32[1024,256]{0,1:T(8,128)S(1)}) fusion(s32[1024]{0:T(1024)S(1)} %iota_add_fusion, s32[256]{0:T(256)S(1)} %iota_add_fusion.1, f32[1024,2]{0,1:T(2,128)S(1)} %bitcast.35, f32[1024,256]{0,1:T(8,128)} %reduce_sum.18, bf16[1024,256]{0,1:T(8,128)(2,1)S(1)} %copy-done, pred[1024]{0:T(1024)(128)(4,1)S(1)} %broadcast_bitcast_fusion.2), kind=kLoop, calls=%fused_computation.8 | loop fusion | flops 2097151 | bytes 2635780 | tf_op jit(solution)/shard_map/reduce_sum | solution.py:72
  163.3 14.6 %psum.28 = f32[]{:T(128)} all-reduce(f32[]{:T(128)} %get-tuple-element.6), channel_id=1, replica_groups=mesh['row'=8,'col_0'=4,'col_1'=4,'layer'=2] {'row'}, use_global_device_ids=true, to_apply=%region_2.3 | all-reduce | flops 1 | bytes 8 | tf_op jit(solution)/shard_map/psum | solution.py:33
  178.0 9.0 %psum.29 = f32[]{:T(128)} all-reduce(f32[]{:T(128)} %psum.28), channel_id=1, replica_groups=mesh['row'=8,'col_0'=4,'col_1'=4,'layer'=2] {'col_0'}, use_global_device_ids=true, to_apply=%region_3.4 | all-reduce | flops 1 | bytes 8 | tf_op jit(solution)/shard_map/psum | solution.py:33
  187.0 7.2 %psum.30 = f32[]{:T(128)} all-reduce(f32[]{:T(128)} %psum.29), channel_id=1, replica_groups=mesh['row'=8,'col_0'=4,'col_1'=4,'layer'=2] {'col_1'}, use_global_device_ids=true, to_apply=%region_4.5 | all-reduce | flops 1 | bytes 8 | tf_op jit(solution)/shard_map/psum | solution.py:33
  194.2 1.3 copy.13
  195.5 10.6 %psum.31 = f32[]{:T(128)} all-reduce(f32[]{:T(128)} %psum.30), channel_id=1, replica_groups=mesh['row'=8,'col_0'=4,'col_1'=4,'layer'=2] {'layer'}, use_global_device_ids=true, to_apply=%region_5.6 | all-reduce | flops 1 | bytes 8 | tf_op jit(solution)/shard_map/psum | solution.py:33
  (16 shorter events, 0.1 us)
Async XLA Ops:
  7.2 61.7 %all-gather.5.cloned.1.call-start = ((), (), s32[]{:S(2)}) async-start(), calls=%async_computation.2 | async-start | bytes 4718592 | tf_op jit(solution)/shard_map/all_gather | solution.py:44
  10.1 135.6 %all-gather.3.cloned.1.call-start = ((), (), s32[]{:S(2)}) async-start(), calls=%async_computation.1 | async-start | bytes 8912896 | tf_op jit(solution)/shard_map/all_gather | solution.py:57
  90.1 11.2 %copy-start.1 = (s32[8,2]{0,1:T(2,128)S(1)}, s32[8,2]{0,1:T(2,128)}, u32[]{:S(2)}) copy-start(s32[8,2]{0,1:T(2,128)} %param.6) | copy-start | bytes 196
  90.1 11.3 %copy-start.2 = (s32[8]{0:T(128)S(1)}, s32[8]{0:T(128)}, u32[]{:S(2)}) copy-start(s32[8]{0:T(128)} %param.7) | copy-start | bytes 100
  100.6 9.8 %collective-permute-start = (bf16[16,256,256]{2,1,0:T(8,128)(2,1)}, bf16[16,256,256]{2,1,0:T(8,128)(2,1)}, u32[]{:S(2)}, u32[]{:S(2)}) collective-permute-start(bf16[16,256,256]{2,1,0:T(8,128)(2,1)} %bitcast.3), channel_id=1, source_target_pairs={{0,1},{1,0},{2,3},{3,2},{4,5},{5,4},{6,7},{7,6},{8,9},{9,8},{10,11... | collective-permute-start | bytes 6291464 | tf_op jit(solution)/shard_map/ppermute | solution.py:17
  154.0 7.1 %copy-start = (bf16[1024,256]{0,1:T(8,128)(2,1)S(1)}, bf16[1024,256]{0,1:T(8,128)(2,1)}, u32[]{:S(2)}) copy-start(bf16[1024,256]{0,1:T(8,128)(2,1)} %bitcast_multiply_fusion) | copy-start | bytes 1572868
Sparse Core Ops, SparseCore 0:
  10.2 58.6 all-gather.4
  71.3 74.3 all-gather.2
where the time goes:
time: 214 us; the launch traced here: 213 us
  waiting for transfers between devices  90.1 us (42%)
  blocking collectives  47.2 us (22%)
  local copies, waits for them, and re-layouts  43.5 us (20%)
  between operations  14.1 us (7%)
  other arithmetic  8.9 us (4%)
  matrix products  8.26 us (4%)
    all_gather x1, waiting for transfers between devices, on_device(): col_panel = lax.all_gather(masked, 'row', axis=0, tiled=True)  58 us
    psum x4, blocking collectives, over_axes(): return functools.reduce(lax.psum, axes, value)  41.4 us
    all_gather x1, waiting for transfers between devices, on_device(): lax.all_gather(masked, COL, axis=1, tiled=True)  31.4 us
    unnamed x14, local copies, waits for them, and re-layouts  22.2 us
    dynamic_slice x1, local copies, waits for them, and re-layouts, on_device(): own_rows = lax.dynamic_index_in_dim(grouped, layer_index, 1, keepdims=False)  13.4 us
    dot_general x1, matrix products, on_device(): jnp.dot(lax.all_gather(masked, COL, axis=1, tiled=True), inner_panel, pre...  8.26 us
    reshape x1, local copies, waits for them, and re-layouts, on_device(): grouped = col_panel.reshape(col_groups, 2, col_width, col_width)  7.82 us
    all_to_all x1, blocking collectives, sum_at_owner(): lax.all_to_all(split_up(value, dim, devices), axis, 0, 0, tiled=True)  5.85 us
  transfers between devices with their start and end apart: 3, of which 2 were waited for; matrix products, arithmetic and copies ran while one was open for 21% of the time, Pallas kernels for 0%

commit v1 on v0

--- a/solution.py
+++ b/solution.py
@@ -9,6 +9,28 @@
 COL = ("col_0", "col_1")
 ROW_COL_LAYER = ("row", "col_0", "col_1", "layer")
 COL_LAYER = ("col_0", "col_1", "layer")
+
+
+def in_order(blocks, dim):
+    shape = list(blocks.shape[1:])
+    shape[dim] *= blocks.shape[0]
+    return jnp.moveaxis(blocks, 0, dim).reshape(shape)
+
+
+def collect(value, axis, dim):
+    devices = lax.axis_size(axis)
+    pairs = [(i, (i + 1) % devices) for i in range(devices)]
+    back = [(b, a) for a, b in pairs]
+    lower, upper = ([], [])
+    for lap in range(devices - 1):
+        if lap % 2 == 0:
+            lower.append(lax.ppermute(lower[-1] if lower else value, axis, pairs))
+        else:
+            upper.append(lax.ppermute(upper[-1] if upper else value, axis, back))
+    parts = jnp.stack([*lower[::-1], value, *upper])
+    shift = lax.axis_index(axis) - len(lower)
+    parts = parts[(jnp.arange(devices) - shift) % devices]
+    return in_order(parts, dim)
 
 
 def partner(value, axis, stride):
@@ -41,7 +63,7 @@
     row_count = density.shape[0]
     col_width = density.shape[1]
     masked = density * expand_mask(block_mask).astype(jnp.bfloat16)
-    col_panel = lax.all_gather(masked, "row", axis=0, tiled=True)
+    col_panel = collect(masked, "row", 0)
     layer_index = lax.axis_index("layer")
     col_groups = lax.axis_size(COL)
     grouped = col_panel.reshape(col_groups, 2, col_width, col_width)

time: 214 us -> 168 us (0.79)
  waiting for transfers between devices: 90.1 us -> 49.5 us
  local copies, waits for them, and re-layouts: 43.5 us -> 26.2 us
  starting transfers between devices: 0.75 us -> 14.5 us
    all_gather x1 -> x0, waiting for transfers between devices: 58 us -> none  [on_device(): col_panel = lax.all_gather(masked, 'row', axis=0, tiled=True)]
    ppermute x0 -> x7, waiting for transfers between devices: none -> 45.5 us  [the longest x4 45.5 us: collect(): lower.append(lax.ppermute(lower[-1] if lower else value, axis, pairs))]
    all_gather x1, waiting for transfers between devices: 31.4 us -> 0.01 us  [on_device(): lax.all_gather(masked, COL, axis=1, tiled=True)]
    unnamed x14 -> x19, local copies, waits for them, and re-layouts: 22.2 us -> 9.76 us
    gather x0 -> x2, local copies, waits for them, and re-layouts: none -> 11.6 us  [collect(): parts = parts[(jnp.arange(devices) - shift) % devices]]
    ppermute x0 -> x7, starting transfers between devices: none -> 10.6 us  [the longest x3 8.1 us: collect(): upper.append(lax.ppermute(upper[-1] if upper else value, axis, back))]
    dynamic_slice x1, local copies, waits for them, and re-layouts: 13.4 us -> 3.97 us  [on_device(): own_rows = lax.dynamic_index_in_dim(grouped, layer_index, 1, keepdims=False)]
    reshape x1 -> x0, local copies, waits for them, and re-layouts: 7.82 us -> none  [on_device(): grouped = col_panel.reshape(col_groups, 2, col_width, col_width)]
  transfers between devices with their start and end apart: 3 -> 9, of which waited for: 2 -> 5; matrix products, arithmetic and copies ran while one was open for 21% -> 16% of each run, Pallas kernels for 0% -> 0%
where the time goes in v1:
time: 168 us; the launch traced here: 167 us
  waiting for transfers between devices  49.5 us (29%)
  blocking collectives  45.6 us (27%)
  local copies, waits for them, and re-layouts  26.2 us (16%)
  starting transfers between devices  14.5 us (9%)
  between operations  14.1 us (8%)
  other arithmetic  9.02 us (5%)
  matrix products  8.26 us (5%)
    ppermute x4, waiting for transfers between devices, collect(): lower.append(lax.ppermute(lower[-1] if lower else value, axis, pairs))  45.5 us
    psum x4, blocking collectives, over_axes(): return functools.reduce(lax.psum, axes, value)  40.2 us
    gather x2, local copies, waits for them, and re-layouts, collect(): parts = parts[(jnp.arange(devices) - shift) % devices]  11.6 us
    unnamed x19, local copies, waits for them, and re-layouts  9.76 us
    dot_general x1, matrix products, on_device(): jnp.dot(lax.all_gather(masked, COL, axis=1, tiled=True), inner_panel, pre...  8.26 us
    ppermute x3, starting transfers between devices, collect(): upper.append(lax.ppermute(upper[-1] if upper else value, axis, back))  8.1 us
    all_to_all x1, blocking collectives, sum_at_owner(): lax.all_to_all(split_up(value, dim, devices), axis, 0, 0, tiled=True)  5.42 us
    dynamic_slice x1, local copies, waits for them, and re-layouts, on_device(): own_rows = lax.dynamic_index_in_dim(grouped, layer_index, 1, keepdims=False)  3.97 us
  transfers between devices with their start and end apart: 9, of which 5 were waited for; matrix products, arithmetic and copies ran while one was open for 16% of the time, Pallas kernels for 0%

profile of v1, /device:TPU:1, one launch (start us, length us, event | category | flops | bytes accessed | tf_op | source)
XLA Modules:
  0.0 167.2 jit_solution(3964422031386870217)
XLA Ops:
  7.2 1.2 copy.10
  10.1 2.5 %collective-permute-start = (bf16[1024,256]{0,1:T(8,128)(2,1)}, bf16[1024,256]{0,1:T(8,128)(2,1)S(1)}, u32[]{:S(2)}, u32[]{:S(2)}) collective-permute-start(bf16[1024,256]{0,1:T(8,128)(2,1)} %bitcast_multiply_fusion), channel_id=1, source_target_pairs={{0,32},{32,64},{64,96},{96,128},{128,160},{160,192},{192,224},{224... | collective-permute-start | bytes 1572872 | tf_op jit(solution)/shard_map/ppermute | solution.py:27
  12.6 15.8 %collective-permute-done = bf16[1024,256]{0,1:T(8,128)(2,1)S(1)} collective-permute-done((bf16[1024,256]{0,1:T(8,128)(2,1)}, bf16[1024,256]{0,1:T(8,128)(2,1)S(1)}, u32[]{:S(2)}, u32[]{:S(2)}) %collective-permute-start) | collective-permute-done | bytes 524320 | tf_op jit(solution)/shard_map/ppermute | solution.py:27
  28.4 2.7 %collective-permute-start.4 = (bf16[1024,256]{0,1:T(8,128)(2,1)}, bf16[1024,256]{0,1:T(8,128)(2,1)S(1)}, u32[]{:S(2)}, u32[]{:S(2)}) collective-permute-start(bf16[1024,256]{0,1:T(8,128)(2,1)} %bitcast_multiply_fusion), channel_id=1, source_target_pairs={{32,0},{64,32},{96,64},{128,96},{160,128},{192,160},{224,192},{0,2... | collective-permute-start | bytes 1572872 | tf_op jit(solution)/shard_map/ppermute | solution.py:29
  31.1 10.8 %collective-permute-done.1 = bf16[1024,256]{0,1:T(8,128)(2,1)S(1)} collective-permute-done((bf16[1024,256]{0,1:T(8,128)(2,1)S(1)}, bf16[1024,256]{0,1:T(8,128)(2,1)S(1)}, u32[]{:S(2)}, u32[]{:S(2)}) %collective-permute-start.1) | collective-permute-done | bytes 524320 | tf_op jit(solution)/shard_map/ppermute | solution.py:27
  41.9 2.7 %collective-permute-start.5 = (bf16[1024,256]{0,1:T(8,128)(2,1)S(1)}, bf16[1024,256]{0,1:T(8,128)(2,1)S(1)}, u32[]{:S(2)}, u32[]{:S(2)}) collective-permute-start(bf16[1024,256]{0,1:T(8,128)(2,1)S(1)} %collective-permute-done.4), channel_id=1, source_target_pairs={{32,0},{64,32},{96,64},{128,96},{160,128},{192,160},{224,192},{0,2... | collective-permute-start | bytes 1572872 | tf_op jit(solution)/shard_map/ppermute | solution.py:29
  44.6 9.9 %collective-permute-done.2 = bf16[1024,256]{0,1:T(8,128)(2,1)S(1)} collective-permute-done((bf16[1024,256]{0,1:T(8,128)(2,1)S(1)}, bf16[1024,256]{0,1:T(8,128)(2,1)S(1)}, u32[]{:S(2)}, u32[]{:S(2)}) %collective-permute-start.2) | collective-permute-done | bytes 524320 | tf_op jit(solution)/shard_map/ppermute | solution.py:27
  54.6 2.7 %collective-permute-start.6 = (bf16[1024,256]{0,1:T(8,128)(2,1)S(1)}, bf16[1024,256]{0,1:T(8,128)(2,1)S(1)}, u32[]{:S(2)}, u32[]{:S(2)}) collective-permute-start(bf16[1024,256]{0,1:T(8,128)(2,1)S(1)} %collective-permute-done.5), channel_id=1, source_target_pairs={{32,0},{64,32},{96,64},{128,96},{160,128},{192,160},{224,192},{0,2... | collective-permute-start | bytes 1572872 | tf_op jit(solution)/shard_map/ppermute | solution.py:29
  57.3 9.0 %collective-permute-done.3 = bf16[1024,256]{0,1:T(8,128)(2,1)} collective-permute-done((bf16[1024,256]{0,1:T(8,128)(2,1)S(1)}, bf16[1024,256]{0,1:T(8,128)(2,1)}, u32[]{:S(2)}, u32[]{:S(2)}) %collective-permute-start.3) | collective-permute-done | bytes 524320 | tf_op jit(solution)/shard_map/ppermute | solution.py:27
  66.3 1.9 %bitcast_dynamic-update-slice_fusion.7 = bf16[8,1024,256]{1,2,0:T(8,128)(2,1)} fusion(bf16[1024,256]{0,1:T(8,128)(2,1)} %collective-permute-done.3), kind=kLoop, calls=%fused_computation.18 | loop fusion | bytes 1048576
  74.2 5.1 %gather_fusion = bf16[8,1024,256]{1,2,0:T(8,128)(2,1)} fusion(bf16[8,1024,256]{1,2,0:T(8,128)(2,1)} %bitcast_dynamic-update-slice_fusion, s32[1024]{0:T(1024)S(1)} %pad_clamp_fusion), kind=kCustom, calls=%fused_computation | custom fusion | bytes 8388640 | tf_op jit(solution)/shard_map/gather | solution.py:32
  79.2 6.5 %copy.11 = bf16[8,1024,256]{2,1,0:T(8,128)(2,1)} copy(bf16[8,1024,256]{1,2,0:T(8,128)(2,1)} %gather_fusion) | data formatting | bytes 8388608 | tf_op jit(solution)/shard_map/gather | solution.py:32
  85.7 4.0 %constant_dynamic-slice_fusion = (bf16[16,1,256,256]{3,2,1,0:T(8,128)(2,1)S(1)}, bf16[16,256,256]{2,1,0:T(8,128)(2,1)}) fusion(bf16[16,2,256,256]{3,2,1,0:T(8,128)(2,1)} %bitcast.52, s32[]{:T(128)S(6)} %select_n.54, s32[]{:T(128)S(6)} %select_n.55), kind=kLoop, calls=%fused_computation.34 | loop fusion | bytes 8388616 | tf_op jit(solution)/shard_map/jit(dynamic_index_in_dim)/dynamic_slice | solution.py:70
  89.7 3.8 %collective-permute-start.7 = (bf16[16,256,256]{2,1,0:T(8,128)(2,1)}, bf16[16,256,256]{2,1,0:T(8,128)(2,1)}, u32[]{:S(2)}, u32[]{:S(2)}) collective-permute-start(bf16[16,256,256]{2,1,0:T(8,128)(2,1)} %get-tuple-element.11), channel_id=1, source_target_pairs={{0,1},{1,0},{2,3},{3,2},{4,5},{5,4},{6,7},{7,6},{8,9},{9,8},{10,11... | collective-permute-start | bytes 6291464 | tf_op jit(solution)/shard_map/ppermute | solution.py:39
  93.8 3.9 %collective-permute-done.7 = bf16[16,256,256]{2,1,0:T(8,128)(2,1)} collective-permute-done((bf16[16,256,256]{2,1,0:T(8,128)(2,1)}, bf16[16,256,256]{2,1,0:T(8,128)(2,1)}, u32[]{:S(2)}, u32[]{:S(2)}) %collective-permute-start.7) | collective-permute-done | bytes 2097184 | tf_op jit(solution)/shard_map/ppermute | solution.py:39
  97.7 3.9 %bitcast_select_fusion.1 = (bf16[4096,256]{1,0:T(8,128)(2,1)}, bf16[4096,256]{1,0:T(8,128)(2,1)}) fusion(bf16[16,256,256]{2,1,0:T(8,128)(2,1)} %collective-permute-done.7, bf16[16,1,256,256]{3,2,1,0:T(8,128)(2,1)S(1)} %get-tuple-element.10, pred[]{:T(512)S(6)} %eq.37), kind=kLoop, calls=%fused_computation.6 | loop fusion | flops 2097152 | bytes 8388609 | tf_op jit(solution)/shard_map/jit(_where)/select_n | solution.py:75
  101.6 8.3 %fusion = f32[1024,512]{0,1:T(8,128)S(1)} fusion(bf16[1024,4096]{0,1:T(8,128)(2,1)} %all-gather.2.cloned.1.call-done, bf16[4096,256]{1,0:T(8,128)(2,1)} %get-tuple-element.9, bf16[4096,256]{1,0:T(8,128)(2,1)} %get-tuple-element.8), kind=kOutput, calls=%fused_computation.1 | convolution fusion | flops 4303355904 | bytes 14680064 | tf_op jit(solution)/shard_map/dot_general | solution.py:78
  109.9 5.4 %all_to_all.5 = f32[2,1024,256]{1,2,0:T(8,128)S(1)} all-to-all(f32[2,1024,256]{1,2,0:T(8,128)S(1)} %bitcast.53), channel_id=1, replica_groups=mesh['row'=8,'col_0'=4,'col_1'=4,'layer'=2] {'layer'}, dimensions={0} | all-to-all | bytes 4194304 | tf_op jit(solution)/shard_map/all_to_all | solution.py:50
  116.5 2.3 %select_reduce_fusion = (f32[]{:T(128)}, f32[1024,256]{0,1:T(8,128)S(1)}) fusion(s32[1024]{0:T(1024)S(1)} %iota_add_fusion, s32[256]{0:T(256)S(1)} %iota_add_fusion.1, f32[1024,2]{0,1:T(2,128)S(1)} %bitcast.54, f32[1024,256]{0,1:T(8,128)} %reduce_sum.18, bf16[1024,256]{0,1:T(8,128)(2,1)S(1)} %copy-done, pred[1024]{0:T(1024)(128)(4,1)S(1)} %broadcast_bitcast_fusion.2), kind=kLoop, calls=%fused_computation.10 | loop fusion | flops 2097151 | bytes 2635780 | tf_op jit(solution)/shard_map/reduce_sum | solution.py:94
  118.8 11.4 %psum.28 = f32[]{:T(128)} all-reduce(f32[]{:T(128)} %get-tuple-element.6), channel_id=1, replica_groups=mesh['row'=8,'col_0'=4,'col_1'=4,'layer'=2] {'row'}, use_global_device_ids=true, to_apply=%region_2.3 | all-reduce | flops 1 | bytes 8 | tf_op jit(solution)/shard_map/psum | solution.py:55
  130.2 9.3 %psum.29 = f32[]{:T(128)} all-reduce(f32[]{:T(128)} %psum.28), channel_id=1, replica_groups=mesh['row'=8,'col_0'=4,'col_1'=4,'layer'=2] {'col_0'}, use_global_device_ids=true, to_apply=%region_3.4 | all-reduce | flops 1 | bytes 8 | tf_op jit(solution)/shard_map/psum | solution.py:55
  139.6 8.9 %psum.30 = f32[]{:T(128)} all-reduce(f32[]{:T(128)} %psum.29), channel_id=1, replica_groups=mesh['row'=8,'col_0'=4,'col_1'=4,'layer'=2] {'col_1'}, use_global_device_ids=true, to_apply=%region_4.5 | all-reduce | flops 1 | bytes 8 | tf_op jit(solution)/shard_map/psum | solution.py:55
  148.5 1.3 copy.12
  149.8 10.5 %psum.31 = f32[]{:T(128)} all-reduce(f32[]{:T(128)} %psum.30), channel_id=1, replica_groups=mesh['row'=8,'col_0'=4,'col_1'=4,'layer'=2] {'layer'}, use_global_device_ids=true, to_apply=%region_5.6 | all-reduce | flops 1 | bytes 8 | tf_op jit(solution)/shard_map/psum | solution.py:55
  (36 shorter events, 9.0 us)
Async XLA Ops:
  7.2 94.5 %all-gather.2.cloned.1.call-start = ((), (), s32[]{:S(2)}) async-start(), calls=%async_computation.1 | async-start | bytes 8912896 | tf_op jit(solution)/shard_map/all_gather | solution.py:79
  10.1 60.7 %copy-start = (bf16[1024,256]{0,1:T(8,128)(2,1)S(1)}, bf16[1024,256]{0,1:T(8,128)(2,1)}, u32[]{:S(2)}) copy-start(bf16[1024,256]{0,1:T(8,128)(2,1)} %bitcast_multiply_fusion) | copy-start | bytes 1572868
  10.1 18.3 %collective-permute-start = (bf16[1024,256]{0,1:T(8,128)(2,1)}, bf16[1024,256]{0,1:T(8,128)(2,1)S(1)}, u32[]{:S(2)}, u32[]{:S(2)}) collective-permute-start(bf16[1024,256]{0,1:T(8,128)(2,1)} %bitcast_multiply_fusion), channel_id=1, source_target_pairs={{0,32},{32,64},{64,96},{96,128},{128,160},{160,192},{192,224},{224... | collective-permute-start | bytes 1572872 | tf_op jit(solution)/shard_map/ppermute | solution.py:27
  28.4 13.5 %collective-permute-start.1 = (bf16[1024,256]{0,1:T(8,128)(2,1)S(1)}, bf16[1024,256]{0,1:T(8,128)(2,1)S(1)}, u32[]{:S(2)}, u32[]{:S(2)}) collective-permute-start(bf16[1024,256]{0,1:T(8,128)(2,1)S(1)} %collective-permute-done), channel_id=1, source_target_pairs={{0,32},{32,64},{64,96},{96,128},{128,160},{160,192},{192,224},{224... | collective-permute-start | bytes 1572872 | tf_op jit(solution)/shard_map/ppermute | solution.py:27
  28.4 13.5 %collective-permute-start.4 = (bf16[1024,256]{0,1:T(8,128)(2,1)}, bf16[1024,256]{0,1:T(8,128)(2,1)S(1)}, u32[]{:S(2)}, u32[]{:S(2)}) collective-permute-start(bf16[1024,256]{0,1:T(8,128)(2,1)} %bitcast_multiply_fusion), channel_id=1, source_target_pairs={{32,0},{64,32},{96,64},{128,96},{160,128},{192,160},{224,192},{0,2... | collective-permute-start | bytes 1572872 | tf_op jit(solution)/shard_map/ppermute | solution.py:29
  41.9 12.6 %collective-permute-start.2 = (bf16[1024,256]{0,1:T(8,128)(2,1)S(1)}, bf16[1024,256]{0,1:T(8,128)(2,1)S(1)}, u32[]{:S(2)}, u32[]{:S(2)}) collective-permute-start(bf16[1024,256]{0,1:T(8,128)(2,1)S(1)} %collective-permute-done.1), channel_id=1, source_target_pairs={{0,32},{32,64},{64,96},{96,128},{128,160},{160,192},{192,224},{224... | collective-permute-start | bytes 1572872 | tf_op jit(solution)/shard_map/ppermute | solution.py:27
  41.9 12.6 %collective-permute-start.5 = (bf16[1024,256]{0,1:T(8,128)(2,1)S(1)}, bf16[1024,256]{0,1:T(8,128)(2,1)S(1)}, u32[]{:S(2)}, u32[]{:S(2)}) collective-permute-start(bf16[1024,256]{0,1:T(8,128)(2,1)S(1)} %collective-permute-done.4), channel_id=1, source_target_pairs={{32,0},{64,32},{96,64},{128,96},{160,128},{192,160},{224,192},{0,2... | collective-permute-start | bytes 1572872 | tf_op jit(solution)/shard_map/ppermute | solution.py:29
  54.5 11.8 %collective-permute-start.3 = (bf16[1024,256]{0,1:T(8,128)(2,1)S(1)}, bf16[1024,256]{0,1:T(8,128)(2,1)}, u32[]{:S(2)}, u32[]{:S(2)}) collective-permute-start(bf16[1024,256]{0,1:T(8,128)(2,1)S(1)} %collective-permute-done.2), channel_id=1, source_target_pairs={{0,32},{32,64},{64,96},{96,128},{128,160},{160,192},{192,224},{224... | collective-permute-start | bytes 1572872 | tf_op jit(solution)/shard_map/ppermute | solution.py:27
  54.6 18.8 %collective-permute-start.6 = (bf16[1024,256]{0,1:T(8,128)(2,1)S(1)}, bf16[1024,256]{0,1:T(8,128)(2,1)S(1)}, u32[]{:S(2)}, u32[]{:S(2)}) collective-permute-start(bf16[1024,256]{0,1:T(8,128)(2,1)S(1)} %collective-permute-done.5), channel_id=1, source_target_pairs={{32,0},{64,32},{96,64},{128,96},{160,128},{192,160},{224,192},{0,2... | collective-permute-start | bytes 1572872 | tf_op jit(solution)/shard_map/ppermute | solution.py:29
  85.7 7.8 %copy-start.1 = (s32[8,2]{0,1:T(2,128)S(1)}, s32[8,2]{0,1:T(2,128)}, u32[]{:S(2)}) copy-start(s32[8,2]{0,1:T(2,128)} %param.6) | copy-start | bytes 196
  85.7 7.9 %copy-start.2 = (s32[8]{0:T(128)S(1)}, s32[8]{0:T(128)}, u32[]{:S(2)}) copy-start(s32[8]{0:T(128)} %param.7) | copy-start | bytes 100
  89.7 8.0 %collective-permute-start.7 = (bf16[16,256,256]{2,1,0:T(8,128)(2,1)}, bf16[16,256,256]{2,1,0:T(8,128)(2,1)}, u32[]{:S(2)}, u32[]{:S(2)}) collective-permute-start(bf16[16,256,256]{2,1,0:T(8,128)(2,1)} %get-tuple-element.11), channel_id=1, source_target_pairs={{0,1},{1,0},{2,3},{3,2},{4,5},{5,4},{6,7},{7,6},{8,9},{9,8},{10,11... | collective-permute-start | bytes 6291464 | tf_op jit(solution)/shard_map/ppermute | solution.py:39
Sparse Core Ops, SparseCore 0:
  11.0 79.5 all-gather.1
